TPU v7x, 512 devices: a whole 4x4x16 slice. The times are simulated.
512 devices in a mesh: ref: 32 (over z, core), qry: 16 (over x, y).
Axes of the slice: x: 4, y: 4, z: 16, core: 2. Of those that a mesh axis runs over, the one named last changes fastest.
Arguments:
- queries: bfloat16 [4096, 1024], P('qry'), may hold values from -1 to 1
- ref_panels: bfloat16 [256, 128, 1024], P('ref', 'qry'), may hold values from -1 to 1
- cand_mask: int32 [32, 256], P('qry', 'ref'), may hold values 0 or 1
- panel_time: int32 [256], replicated, may hold values from 0 to 255, as said below
- w_first: float32 [9, 32], replicated, may hold values from -2 to 2
- b_first: float32 [32], replicated, may hold values from -2.5 to 2.5
- w_second: bfloat16 [9, 32], replicated, may hold values from -0.375 to 0.375
Outputs:
- score_map: bfloat16 [4096, 32768], P('qry', 'ref')
Inputs may be any that keep to these rules, and one draw needn't show every extreme that they name: `panel_time`: A permutation of the reference time blocks. The owner of block t is t // 8; every owner has 8 blocks. The 8 panels of one ingest index of ref (panels held by one index) include at most 1 of one owner, and every ingest index has 1 panel of some owner.
All inputs are finite; a program needn't handle non-finite values. No bound on the sum of `cand_mask` on one device may be relied on, other than what follows from the above.
Results may differ from a plain program's by a relative error of at most 0.0059.
Values may be sent and summed in bfloat16 or wider, within the bound.
No kernel may reach another device: no remote copies, remote signals or barrier semaphores. Data moves between devices by JAX's collectives and lax.ppermute only.
A program may use at most 64 MiB of HBM per device.

v0:
```python
import math
import jax
import jax.numpy as jnp
from jax import lax
from jax.sharding import PartitionSpec as P

FRAMES = 256


def with_halo(cells, sides, width):
    for axis, dim in sides:
        count = lax.axis_size(axis)
        ends = count - 1
        head = lax.slice_in_dim(cells, 0, width, axis=dim)
        tail = lax.slice_in_dim(cells, cells.shape[dim] - width, cells.shape[dim], axis=dim)
        cells = jnp.concatenate(
            [
                lax.ppermute(tail, axis, [(i, (i + 1) % count) for i in range(ends)]),
                cells,
                lax.ppermute(head, axis, [((i + 1) % count, i) for i in range(ends)]),
            ],
            axis=dim,
        )
    return cells


def layer_one(strip_cols, w_first, b_first):
    height = strip_cols.shape[0]
    widths = strip_cols.shape[1] - 2
    padded = jnp.pad(strip_cols.astype(jnp.float32), ((1, 1), (0, 0)))
    summed = jnp.broadcast_to(b_first[:, None, None], (b_first.shape[0], height, widths))
    for row_shift in range(3):
        for col_shift in range(3):
            summed = (
                summed
                + w_first[3 * row_shift + col_shift][:, None, None]
                * padded[row_shift : row_shift + height, col_shift : col_shift + widths][None]
            )
    return jnp.maximum(summed, 0.0).astype(jnp.bfloat16)


def layer_two(hidden, w_second):
    height = hidden.shape[1]
    widths = hidden.shape[2] - 2
    padded = jnp.pad(hidden, ((0, 0), (1, 1), (0, 0)))
    summed = jnp.zeros((height, widths), jnp.float32)
    for row_shift in range(3):
        for col_shift in range(3):
            summed = summed + jnp.einsum(
                "c,chw->hw",
                w_second[3 * row_shift + col_shift],
                padded[:, row_shift : row_shift + height, col_shift : col_shift + widths],
                preferred_element_type=jnp.float32,
            )
    return summed


def shards(queries, ref_panels, cand_mask, panel_time, w_first, b_first, w_second):
    owners_count = lax.axis_size("ref")
    my_owner = lax.axis_index("ref")
    blocks_dev = ref_panels.shape[0]
    frames_dev = queries.shape[0]
    videos = frames_dev // FRAMES
    slot_count = max(1, (2 * blocks_dev + owners_count - 1) // owners_count)
    times = panel_time.reshape(owners_count, blocks_dev)
    owner_ids = times // blocks_dev
    within = times % blocks_dev
    earlier = jnp.arange(blocks_dev)[None, :] < jnp.arange(blocks_dev)[:, None]
    same_owner = owner_ids[:, :, None] == owner_ids[:, None, :]
    ranks = jnp.sum((same_owner & earlier[None]).astype(jnp.int32), axis=2)
    owner_mine = lax.dynamic_index_in_dim(owner_ids, my_owner, 0, keepdims=False)
    rank_mine = lax.dynamic_index_in_dim(ranks, my_owner, 0, keepdims=False)
    dest_ids = jnp.arange(owners_count)
    slot_ids = jnp.arange(slot_count)
    select = (
        (owner_mine[None, None, :] == dest_ids[:, None, None])
        & (rank_mine[None, None, :] == slot_ids[None, :, None])
    ).astype(jnp.bfloat16)
    outgoing = jnp.einsum(
        "oki,ird->okrd", select, ref_panels, preferred_element_type=jnp.float32
    ).astype(jnp.bfloat16)
    incoming = lax.all_to_all(outgoing, "ref", split_axis=0, concat_axis=0, tiled=True)
    placing = (
        (owner_ids == my_owner)[None, :, None, :]
        & (ranks[None, :, None, :] == slot_ids[None, None, :, None])
        & (within[None, :, None, :] == jnp.arange(blocks_dev)[:, None, None, None])
    )
    placement = jnp.sum(placing.astype(jnp.int32), axis=3).astype(jnp.bfloat16)
    owned = jnp.einsum(
        "tsk,skrd->trd", placement, incoming, preferred_element_type=jnp.float32
    ).astype(jnp.bfloat16)
    tiles = jnp.einsum(
        "qd,brd->qbr",
        queries,
        lax.all_gather(owned, "qry", axis=1, tiled=True),
        preferred_element_type=jnp.float32,
    ).astype(jnp.bfloat16)
    panel_len = tiles.shape[2]
    ref_cols = blocks_dev * panel_len
    qblock_count = cand_mask.shape[0]
    keeper = cand_mask.astype(jnp.bfloat16)[:, None, :, None]
    sims = (
        tiles.reshape(qblock_count, frames_dev // qblock_count, blocks_dev, panel_len) * keeper
    ).reshape(videos, FRAMES, ref_cols)
    first_layer = jax.vmap(layer_one, in_axes=(0, None, None))
    second_layer = jax.vmap(layer_two, in_axes=(0, None))
    single = with_halo(sims, (("ref", 2),), 1)
    spread = jnp.pad(single, ((0, 0), (0, 0), (1, 1)))
    first_col = first_layer(spread[:, :, 1:4], w_first, b_first)[:, :, :, 0]
    last_col = first_layer(spread[:, :, ref_cols : ref_cols + 3], w_first, b_first)[:, :, :, 0]
    edge_pair = jnp.stack([first_col, last_col])
    near_cols = with_halo(edge_pair, (("ref", 0),), 1)
    left_fill = near_cols[0]
    right_fill = near_cols[3]
    left_use = my_owner >= 0
    right_use = my_owner >= 0
    block_cols = math.gcd(256, ref_cols)
    count = ref_cols // block_cols

    def one_block(block_index):
        strip_cols = lax.dynamic_slice_in_dim(spread, block_index * block_cols, block_cols + 4, 2)
        hidden = first_layer(strip_cols, w_first, b_first)
        first = jnp.where((block_index == 0) & left_use, left_fill, hidden[:, :, :, 0])
        final = jnp.where((block_index == count - 1) & right_use, right_fill, hidden[:, :, :, -1])
        hidden = hidden.at[:, :, :, 0].set(first).at[:, :, :, -1].set(final)
        return second_layer(hidden, w_second).astype(jnp.bfloat16)

    blocks_out = lax.map(one_block, jnp.arange(count, dtype=jnp.int32))
    return jnp.transpose(blocks_out, (1, 2, 0, 3)).reshape(frames_dev, ref_cols)


def solution(mesh):
    placed = (P("qry", None), P("ref", "qry", None), P("qry", "ref"), P(), P(), P(), P())
    return jax.shard_map(
        shards, mesh=mesh, in_specs=placed, out_specs=P("qry", "ref"), check_vma=False
    )
```

profile of v0, /device:TPU:97, one launch (start us, length us, event | category | flops | bytes accessed | tf_op | source)
XLA Modules:
  0.0 401.1 jit_solution(5966374788965295155)
XLA Ops:
  10.3 14.8 %all-to-all-start = ((bf16[32,1,8,1024]{3,2,1,0:T(8,128)(2,1)}), bf16[32,1,8,1024]{3,2,1,0:T(8,128)(2,1)S(1)}, u32[]{:S(2)}, u32[]{:S(2)}) async-start(bf16[32,1,8,1024]{3,2,1,0:T(8,128)(2,1)} %copy.95), calls=%async_computation | async-start | bytes 1048576 | tf_op jit(solution)/shard_map/all_to_all | solution.py:82
  25.2 30.0 %all-to-all-done = bf16[32,1,8,1024]{3,2,1,0:T(8,128)(2,1)S(1)} async-done(((bf16[32,1,8,1024]{3,2,1,0:T(8,128)(2,1)}), bf16[32,1,8,1024]{3,2,1,0:T(8,128)(2,1)S(1)}, u32[]{:S(2)}, u32[]{:S(2)}) %all-to-all-start) | async-done | bytes 524320 | tf_op jit(solution)/shard_map/all_to_all | solution.py:82
  57.5 53.4 %all-gather.2.cloned.1.call-done = bf16[8,128,1024]{2,0,1:T(8,128)(2,1)} async-done(((bf16[8,8,1024]{2,0,1:T(8,128)(2,1)}), bf16[8,128,1024]{2,0,1:T(8,128)(2,1)}) %all-gather.2.cloned.1.call-update) | async-done | bytes 2097168 | tf_op jit(solution)/shard_map/all_gather | solution.py:95
  110.9 4.0 fusion.52
  115.4 5.8 %collective-permute-start = (bf16[1,256,1]{2,1,0:T(8,128)(2,1)S(1)}, bf16[1,256,1]{2,1,0:T(8,128)(2,1)S(1)}, u32[]{:S(2)}, u32[]{:S(2)}) collective-permute-start(bf16[1,256,1]{2,1,0:T(8,128)(2,1)S(1)} %get-tuple-element.254), channel_id=1, source_target_pairs={{0,16},{16,32},{32,48},{48,64},{64,80},{80,96},{96,112},{112,128},... | collective-permute-start | bytes 1544 | tf_op jit(solution)/shard_map/ppermute | solution.py:18
  123.2 4.8 %collective-permute-done.1 = bf16[1,256,1]{2,1,0:T(8,128)(2,1)S(1)} collective-permute-done((bf16[1,256,1]{2,1,0:T(8,128)(2,1)S(1)}, bf16[1,256,1]{2,1,0:T(8,128)(2,1)S(1)}, u32[]{:S(2)}, u32[]{:S(2)}) %collective-permute-start.1) | collective-permute-done | bytes 544 | tf_op jit(solution)/shard_map/ppermute | solution.py:20
  132.8 4.9 %collective-permute-start.2 = (bf16[1,1,32,256]{3,2,1,0:T(8,128)(2,1)S(1)}, bf16[1,1,32,256]{3,2,1,0:T(8,128)(2,1)}, u32[]{:S(2)}, u32[]{:S(2)}) collective-permute-start(bf16[1,1,32,256]{3,2,1,0:T(8,128)(2,1)S(1)} %maximum_convert_fusion.2), channel_id=1, source_target_pairs={{0,16},{16,32},{32,48},{48,64},{64,80},{80,96},{96,112},{112,128},... | collective-permute-start | bytes 49160 | tf_op jit(solution)/shard_map/ppermute | solution.py:18
  140.0 251.9 %while.15 = (s32[]{:T(128)}, bf16[4,1,256,256]{3,2,1,0:T(8,128)(2,1)}, f32[32]{0:T(128)}, f32[9,32]{1,0:T(8,128)S(1)}, s32[4]{0:T(128)}, /*index=5*/bf16[1,256,1...) while((s32[]{:T(128)}, ...), condition=%wide.region_3.4_spmd, body=%wide.region_2.3_spmd.sunk | while | flops 80692224 | bytes 88695848 | solution.py:128
  149.3 14.2 %maximum_convert_fusion.4 = bf16[1,32,256,258]{2,1,3,0:T(8,128)(2,1)S(1)} fusion(f32[256,258]{0,1:T(8,128)S(1)} %copy.138, f32[32]{0:T(128)S(1)} %get-tuple-element.355, f32[256,258]{0,1:T(8,128)} %copy.139, f32[32]{0:T(128)S(1)} %get-tuple-element.357, f32[256,258]{0,1:T(8,128)} %copy.140, f32[32]{0:T(128)S(1)} %get-tuple-element.359, ...), kind=kLoop, calls=%fused_computation.clone.1 | loop fusion | flops 42270720 | bytes 6606080 | tf_op jit(solution)/shard_map/while/body/eval_jaxpr/vmap()/convert_element_type | solution.py:39
  170.8 3.6 fusion.118
  174.5 3.6 fusion.119
  178.2 3.6 fusion.120
  181.9 2.8 fusion.121
  184.9 2.8 fusion.122
  187.9 2.8 fusion.123
  190.9 3.6 fusion.124
  194.7 3.6 fusion.125
  198.4 3.6 fusion.126
  212.3 14.2 %maximum_convert_fusion.4 = bf16[1,32,256,258]{2,1,3,0:T(8,128)(2,1)S(1)} fusion(f32[256,258]{0,1:T(8,128)S(1)} %copy.138, f32[32]{0:T(128)S(1)} %get-tuple-element.355, f32[256,258]{0,1:T(8,128)} %copy.139, f32[32]{0:T(128)S(1)} %get-tuple-element.357, f32[256,258]{0,1:T(8,128)} %copy.140, f32[32]{0:T(128)S(1)} %get-tuple-element.359, ...), kind=kLoop, calls=%fused_computation.clone.1 | loop fusion | flops 42270720 | bytes 6606080 | tf_op jit(solution)/shard_map/while/body/eval_jaxpr/vmap()/convert_element_type | solution.py:39
  233.8 3.6 fusion.118
  237.5 3.6 fusion.119
  241.2 3.6 fusion.120
  244.9 2.8 fusion.121
  247.9 2.8 fusion.122
  250.9 2.8 fusion.123
  253.9 3.6 fusion.124
  257.7 3.6 fusion.125
  261.4 3.6 fusion.126
  275.2 14.2 %maximum_convert_fusion.4 = bf16[1,32,256,258]{2,1,3,0:T(8,128)(2,1)S(1)} fusion(f32[256,258]{0,1:T(8,128)S(1)} %copy.138, f32[32]{0:T(128)S(1)} %get-tuple-element.355, f32[256,258]{0,1:T(8,128)} %copy.139, f32[32]{0:T(128)S(1)} %get-tuple-element.357, f32[256,258]{0,1:T(8,128)} %copy.140, f32[32]{0:T(128)S(1)} %get-tuple-element.359, ...), kind=kLoop, calls=%fused_computation.clone.1 | loop fusion | flops 42270720 | bytes 6606080 | tf_op jit(solution)/shard_map/while/body/eval_jaxpr/vmap()/convert_element_type | solution.py:39
  296.8 3.6 fusion.118
  300.5 3.6 fusion.119
  304.2 3.6 fusion.120
  307.9 2.8 fusion.121
  310.9 2.8 fusion.122
  313.9 2.8 fusion.123
  316.9 3.6 fusion.124
  320.7 3.6 fusion.125
  324.4 3.6 fusion.126
  338.2 14.2 %maximum_convert_fusion.4 = bf16[1,32,256,258]{2,1,3,0:T(8,128)(2,1)S(1)} fusion(f32[256,258]{0,1:T(8,128)S(1)} %copy.138, f32[32]{0:T(128)S(1)} %get-tuple-element.355, f32[256,258]{0,1:T(8,128)} %copy.139, f32[32]{0:T(128)S(1)} %get-tuple-element.357, f32[256,258]{0,1:T(8,128)} %copy.140, f32[32]{0:T(128)S(1)} %get-tuple-element.359, ...), kind=kLoop, calls=%fused_computation.clone.1 | loop fusion | flops 42270720 | bytes 6606080 | tf_op jit(solution)/shard_map/while/body/eval_jaxpr/vmap()/convert_element_type | solution.py:39
  359.7 3.6 fusion.118
  363.5 3.6 fusion.119
  367.2 3.6 fusion.120
  370.9 2.8 fusion.121
  373.9 2.8 fusion.122
  376.9 2.8 fusion.123
  379.9 3.6 fusion.124
  383.6 3.6 fusion.125
  387.4 3.6 fusion.126
  (160 shorter events, 83.9 us)
Async XLA Ops:
  6.5 104.4 %copy-start = (bf16[256,1024]{1,0:T(8,128)(2,1)S(1)}, bf16[256,1024]{1,0:T(8,128)(2,1)}, u32[]{:S(2)}) copy-start(bf16[256,1024]{1,0:T(8,128)(2,1)} %param.13) | copy-start | bytes 1572868
  10.3 44.8 %all-to-all-start = ((bf16[32,1,8,1024]{3,2,1,0:T(8,128)(2,1)}), bf16[32,1,8,1024]{3,2,1,0:T(8,128)(2,1)S(1)}, u32[]{:S(2)}, u32[]{:S(2)}) async-start(bf16[32,1,8,1024]{3,2,1,0:T(8,128)(2,1)} %copy.95), calls=%async_computation | async-start | bytes 1048576 | tf_op jit(solution)/shard_map/all_to_all | solution.py:82
  25.1 85.8 %all-gather.2.cloned.1.call-start = ((), (), s32[]{:S(2)}) async-start(), calls=%async_computation.1 | async-start | bytes 2228224 | tf_op jit(solution)/shard_map/all_gather | solution.py:95
  57.3 65.9 %copy-start.2 = (f32[9,32]{1,0:T(8,128)S(1)}, f32[9,32]{1,0:T(8,128)}, u32[]{:S(2)}) copy-start(f32[9,32]{1,0:T(8,128)} %param.17) | copy-start | bytes 3460
  115.4 7.7 %collective-permute-start = (bf16[1,256,1]{2,1,0:T(8,128)(2,1)S(1)}, bf16[1,256,1]{2,1,0:T(8,128)(2,1)S(1)}, u32[]{:S(2)}, u32[]{:S(2)}) collective-permute-start(bf16[1,256,1]{2,1,0:T(8,128)(2,1)S(1)} %get-tuple-element.254), channel_id=1, source_target_pairs={{0,16},{16,32},{32,48},{48,64},{64,80},{80,96},{96,112},{112,128},... | collective-permute-start | bytes 1544 | tf_op jit(solution)/shard_map/ppermute | solution.py:18
  121.2 6.8 %collective-permute-start.1 = (bf16[1,256,1]{2,1,0:T(8,128)(2,1)S(1)}, bf16[1,256,1]{2,1,0:T(8,128)(2,1)S(1)}, u32[]{:S(2)}, u32[]{:S(2)}) collective-permute-start(bf16[1,256,1]{2,1,0:T(8,128)(2,1)S(1)} %get-tuple-element.253), channel_id=1, source_target_pairs={{16,0},{32,16},{48,32},{64,48},{80,64},{96,80},{112,96},{128,112},... | collective-permute-start | bytes 1544 | tf_op jit(solution)/shard_map/ppermute | solution.py:20
  130.1 9.3 %collective-permute-start.3 = (bf16[1,1,32,256]{3,2,1,0:T(8,128)(2,1)S(1)}, bf16[1,1,32,256]{3,2,1,0:T(8,128)(2,1)}, u32[]{:S(2)}, u32[]{:S(2)}) collective-permute-start(bf16[1,1,32,256]{3,2,1,0:T(8,128)(2,1)S(1)} %maximum_convert_fusion.1), channel_id=1, source_target_pairs={{16,0},{32,16},{48,32},{64,48},{80,64},{96,80},{112,96},{128,112},... | collective-permute-start | bytes 49160 | tf_op jit(solution)/shard_map/ppermute | solution.py:20
  132.8 6.6 %collective-permute-start.2 = (bf16[1,1,32,256]{3,2,1,0:T(8,128)(2,1)S(1)}, bf16[1,1,32,256]{3,2,1,0:T(8,128)(2,1)}, u32[]{:S(2)}, u32[]{:S(2)}) collective-permute-start(bf16[1,1,32,256]{3,2,1,0:T(8,128)(2,1)S(1)} %maximum_convert_fusion.2), channel_id=1, source_target_pairs={{0,16},{16,32},{32,48},{48,64},{64,80},{80,96},{96,112},{112,128},... | collective-permute-start | bytes 49160 | tf_op jit(solution)/shard_map/ppermute | solution.py:18
  163.5 3.2 copy-start.1
  163.5 7.3 %copy-start.3 = (bf16[9,32]{1,0:T(8,128)(2,1)S(1)}, bf16[9,32]{1,0:T(8,128)(2,1)}, u32[]{:S(2)}) copy-start(bf16[9,32]{1,0:T(8,128)(2,1)} %get-tuple-element.413) | copy-start | bytes 1732 | tf_op jit(solution)/shard_map/while
  226.5 3.2 copy-start.1
  226.5 7.3 %copy-start.3 = (bf16[9,32]{1,0:T(8,128)(2,1)S(1)}, bf16[9,32]{1,0:T(8,128)(2,1)}, u32[]{:S(2)}) copy-start(bf16[9,32]{1,0:T(8,128)(2,1)} %get-tuple-element.413) | copy-start | bytes 1732 | tf_op jit(solution)/shard_map/while
  289.5 3.2 copy-start.1
  289.5 7.3 %copy-start.3 = (bf16[9,32]{1,0:T(8,128)(2,1)S(1)}, bf16[9,32]{1,0:T(8,128)(2,1)}, u32[]{:S(2)}) copy-start(bf16[9,32]{1,0:T(8,128)(2,1)} %get-tuple-element.413) | copy-start | bytes 1732 | tf_op jit(solution)/shard_map/while
  352.4 3.2 copy-start.1
  352.5 7.3 %copy-start.3 = (bf16[9,32]{1,0:T(8,128)(2,1)S(1)}, bf16[9,32]{1,0:T(8,128)(2,1)}, u32[]{:S(2)}) copy-start(bf16[9,32]{1,0:T(8,128)(2,1)} %get-tuple-element.413) | copy-start | bytes 1732 | tf_op jit(solution)/shard_map/while
Sparse Core Ops, SparseCore 0:
  56.6 54.2 all-gather.1
where the time goes:
time: 404 us; the launch traced here: 401 us
  matrix products  127 us (31%)
  waiting for transfers between devices  88.2 us (22%)
  other arithmetic  78.1 us (19%)
  local copies, waits for them, and re-layouts  56.3 us (14%)
  starting transfers between devices  29.3 us (7%)
  between operations  13.6 us (3%)
  loops' own time  8.92 us (2%)
    dot_general x36, matrix products, layer_two(): jnp.einsum('c,chw->hw', w_second[3 * row_shift + col_shift], padded[:, ro...  120 us
    convert_element_type x6, other arithmetic, layer_one(): return jnp.maximum(summed, 0.0).astype(jnp.bfloat16)  58.4 us
    all_gather x1, waiting for transfers between devices, shards(): lax.all_gather(owned, 'qry', axis=1, tiled=True)  53.4 us
    all_to_all x1, waiting for transfers between devices, shards(): lax.all_to_all(outgoing, 'ref', split_axis=0, concat_axis=0, tiled=True)  30 us
    mul x44, local copies, waits for them, and re-layouts, layer_one(): w_first[3 * row_shift + col_shift][:, None, None]  24.6 us
    all_to_all x1, starting transfers between devices, shards(): lax.all_to_all(outgoing, 'ref', split_axis=0, concat_axis=0, tiled=True)  14.8 us
    while x20, local copies, waits for them, and re-layouts  12.8 us
    scatter x8, other arithmetic, one_block(): hidden = hidden.at[:, :, :, 0].set(first).at[:, :, :, -1].set(final)  10.9 us
  transfers between devices with their start and end apart: 6, of which 3 were waited for; matrix products, arithmetic and copies ran while one was open for 1% of the time, Pallas kernels for 0%

commit v1 on v0

--- a/solution.py
+++ b/solution.py
@@ -5,6 +5,13 @@
 from jax.sharding import PartitionSpec as P
 
 FRAMES = 256
+
+
+def gather_over(block, mesh_axis, d):
+    count = lax.axis_size(mesh_axis)
+    blocks = jnp.stack([block for _ in range(count)])
+    blocks = lax.all_to_all(blocks, mesh_axis, split_axis=0, concat_axis=0)
+    return jnp.concatenate(blocks, axis=d)
 
 
 def with_halo(cells, sides, width):
@@ -90,10 +97,7 @@
         "tsk,skrd->trd", placement, incoming, preferred_element_type=jnp.float32
     ).astype(jnp.bfloat16)
     tiles = jnp.einsum(
-        "qd,brd->qbr",
-        queries,
-        lax.all_gather(owned, "qry", axis=1, tiled=True),
-        preferred_element_type=jnp.float32,
+        "qd,brd->qbr", queries, gather_over(owned, "qry", 1), preferred_element_type=jnp.float32
     ).astype(jnp.bfloat16)
     panel_len = tiles.shape[2]
     ref_cols = blocks_dev * panel_len

time: 404 us -> 371 us (0.918)
  the two profiles are of different devices: /device:TPU:97 before, /device:TPU:1 now
where the time goes in v1:
time: 371 us; the launch traced here: 368 us
  matrix products  124 us (33%)
  other arithmetic  77.4 us (21%)
  waiting for transfers between devices  64.5 us (17%)
  local copies, waits for them, and re-layouts  57.9 us (16%)
  starting transfers between devices  35 us (9%)
  loops' own time  8.92 us (2%)
    dot_general x36, matrix products, layer_two(): jnp.einsum('c,chw->hw', w_second[3 * row_shift + col_shift], padded[:, ro...  120 us
    convert_element_type x6, other arithmetic, layer_one(): return jnp.maximum(summed, 0.0).astype(jnp.bfloat16)  58.4 us
    all_to_all x1, waiting for transfers between devices, shards(): lax.all_to_all(outgoing, 'ref', split_axis=0, concat_axis=0, tiled=True)  33.5 us
    all_to_all x1, waiting for transfers between devices, gather_over(): blocks = lax.all_to_all(blocks, mesh_axis, split_axis=0, concat_axis=0)  28.7 us
    mul x44, local copies, waits for them, and re-layouts, layer_one(): w_first[3 * row_shift + col_shift][:, None, None]  24.6 us
    all_to_all x1, starting transfers between devices, shards(): lax.all_to_all(outgoing, 'ref', split_axis=0, concat_axis=0, tiled=True)  16.9 us
    while x20, local copies, waits for them, and re-layouts  12.8 us
    scatter x8, other arithmetic, one_block(): hidden = hidden.at[:, :, :, 0].set(first).at[:, :, :, -1].set(final)  10.9 us
  transfers between devices with their start and end apart: 6, of which 3 were waited for; matrix products, arithmetic and copies ran while one was open for 1% of the time, Pallas kernels for 0%

profile of v1, /device:TPU:1, one launch (start us, length us, event | category | flops | bytes accessed | tf_op | source)
XLA Modules:
  0.0 368.3 jit_solution(2649008010921877142)
XLA Ops:
  3.8 16.9 %all-to-all-start = ((bf16[32,1,8,1024]{3,2,1,0:T(8,128)(2,1)}), bf16[32,1,8,1024]{3,2,1,0:T(8,128)(2,1)S(1)}, u32[]{:S(2)}, u32[]{:S(2)}) async-start(bf16[32,1,8,1024]{3,2,1,0:T(8,128)(2,1)} %copy.84), calls=%async_computation | async-start | bytes 1048576 | tf_op jit(solution)/shard_map/all_to_all | solution.py:89
  20.7 33.5 %all-to-all-done = bf16[32,1,8,1024]{3,2,1,0:T(8,128)(2,1)S(1)} async-done(((bf16[32,1,8,1024]{3,2,1,0:T(8,128)(2,1)}), bf16[32,1,8,1024]{3,2,1,0:T(8,128)(2,1)S(1)}, u32[]{:S(2)}, u32[]{:S(2)}) %all-to-all-start) | async-done | bytes 524320 | tf_op jit(solution)/shard_map/all_to_all | solution.py:89
  56.5 6.8 %all-to-all-start.1 = ((bf16[16,8,8,1024]{3,2,1,0:T(8,128)(2,1)}), bf16[16,8,8,1024]{3,2,1,0:T(8,128)(2,1)}, u32[]{:S(2)}, u32[]{:S(2)}) async-start(bf16[16,8,8,1024]{3,2,1,0:T(8,128)(2,1)} %stack.2), calls=%async_computation.1 | async-start | bytes 4194304 | tf_op jit(solution)/shard_map/all_to_all | solution.py:13
  63.7 28.7 %all-to-all-done.1 = bf16[16,8,8,1024]{3,2,1,0:T(8,128)(2,1)} async-done(((bf16[16,8,8,1024]{3,2,1,0:T(8,128)(2,1)}), bf16[16,8,8,1024]{3,2,1,0:T(8,128)(2,1)}, u32[]{:S(2)}, u32[]{:S(2)}) %all-to-all-start.1) | async-done | bytes 2097184 | tf_op jit(solution)/shard_map/all_to_all | solution.py:13
  95.2 2.5 collective-permute-start
  97.7 3.2 collective-permute-start.1
  108.1 3.6 collective-permute-start.2
  114.1 251.9 %while.15 = (s32[]{:T(128)}, bf16[4,1,256,256]{3,2,1,0:T(8,128)(2,1)}, f32[32]{0:T(128)}, f32[9,32]{1,0:T(8,128)S(1)}, s32[4]{0:T(128)}, /*index=5*/bf16[1,256,1...) while((s32[]{:T(128)}, ...), condition=%wide.region_3.4_spmd, body=%wide.region_2.3_spmd.sunk | while | flops 80692224 | bytes 88695848 | solution.py:132
  123.3 14.2 %maximum_convert_fusion.4 = bf16[1,32,256,258]{2,1,3,0:T(8,128)(2,1)S(1)} fusion(f32[256,258]{0,1:T(8,128)S(1)} %copy.130, f32[32]{0:T(128)S(1)} %get-tuple-element.355, f32[256,258]{0,1:T(8,128)} %copy.131, f32[32]{0:T(128)S(1)} %get-tuple-element.357, f32[256,258]{0,1:T(8,128)} %copy.132, f32[32]{0:T(128)S(1)} %get-tuple-element.359, ...), kind=kLoop, calls=%fused_computation.clone.1 | loop fusion | flops 42270720 | bytes 6606080 | tf_op jit(solution)/shard_map/while/body/eval_jaxpr/vmap()/convert_element_type | solution.py:46
  144.9 3.6 fusion.120
  148.6 3.6 fusion.121
  152.3 3.6 fusion.122
  156.0 2.8 fusion.123
  159.0 2.8 fusion.124
  162.0 2.8 fusion.125
  165.0 3.6 fusion.126
  168.8 3.6 fusion.127
  172.5 3.6 fusion.128
  186.3 14.2 %maximum_convert_fusion.4 = bf16[1,32,256,258]{2,1,3,0:T(8,128)(2,1)S(1)} fusion(f32[256,258]{0,1:T(8,128)S(1)} %copy.130, f32[32]{0:T(128)S(1)} %get-tuple-element.355, f32[256,258]{0,1:T(8,128)} %copy.131, f32[32]{0:T(128)S(1)} %get-tuple-element.357, f32[256,258]{0,1:T(8,128)} %copy.132, f32[32]{0:T(128)S(1)} %get-tuple-element.359, ...), kind=kLoop, calls=%fused_computation.clone.1 | loop fusion | flops 42270720 | bytes 6606080 | tf_op jit(solution)/shard_map/while/body/eval_jaxpr/vmap()/convert_element_type | solution.py:46
  207.9 3.6 fusion.120
  211.6 3.6 fusion.121
  215.3 3.6 fusion.122
  219.0 2.8 fusion.123
  222.0 2.8 fusion.124
  225.0 2.8 fusion.125
  228.0 3.6 fusion.126
  231.7 3.6 fusion.127
  235.5 3.6 fusion.128
  249.3 14.2 %maximum_convert_fusion.4 = bf16[1,32,256,258]{2,1,3,0:T(8,128)(2,1)S(1)} fusion(f32[256,258]{0,1:T(8,128)S(1)} %copy.130, f32[32]{0:T(128)S(1)} %get-tuple-element.355, f32[256,258]{0,1:T(8,128)} %copy.131, f32[32]{0:T(128)S(1)} %get-tuple-element.357, f32[256,258]{0,1:T(8,128)} %copy.132, f32[32]{0:T(128)S(1)} %get-tuple-element.359, ...), kind=kLoop, calls=%fused_computation.clone.1 | loop fusion | flops 42270720 | bytes 6606080 | tf_op jit(solution)/shard_map/while/body/eval_jaxpr/vmap()/convert_element_type | solution.py:46
  270.9 3.6 fusion.120
  274.6 3.6 fusion.121
  278.3 3.6 fusion.122
  282.0 2.8 fusion.123
  285.0 2.8 fusion.124
  288.0 2.8 fusion.125
  291.0 3.6 fusion.126
  294.7 3.6 fusion.127
  298.5 3.6 fusion.128
  312.3 14.2 %maximum_convert_fusion.4 = bf16[1,32,256,258]{2,1,3,0:T(8,128)(2,1)S(1)} fusion(f32[256,258]{0,1:T(8,128)S(1)} %copy.130, f32[32]{0:T(128)S(1)} %get-tuple-element.355, f32[256,258]{0,1:T(8,128)} %copy.131, f32[32]{0:T(128)S(1)} %get-tuple-element.357, f32[256,258]{0,1:T(8,128)} %copy.132, f32[32]{0:T(128)S(1)} %get-tuple-element.359, ...), kind=kLoop, calls=%fused_computation.clone.1 | loop fusion | flops 42270720 | bytes 6606080 | tf_op jit(solution)/shard_map/while/body/eval_jaxpr/vmap()/convert_element_type | solution.py:46
  333.8 3.6 fusion.120
  337.5 3.6 fusion.121
  341.3 3.6 fusion.122
  345.0 2.8 fusion.123
  348.0 2.8 fusion.124
  351.0 2.8 fusion.125
  354.0 3.6 fusion.126
  357.7 3.6 fusion.127
  361.4 3.6 fusion.128
  (163 shorter events, 86.9 us)
Async XLA Ops:
  0.0 92.4 %copy-start = (bf16[256,1024]{1,0:T(8,128)(2,1)S(1)}, bf16[256,1024]{1,0:T(8,128)(2,1)}, u32[]{:S(2)}) copy-start(bf16[256,1024]{1,0:T(8,128)(2,1)} %param.13) | copy-start | bytes 1572868
  3.8 59.5 %copy-start.4 = (s32[2,8]{1,0:T(2,128)S(1)}, s32[2,8]{1,0:T(2,128)}, u32[]{:S(2)}) copy-start(s32[2,8]{1,0:T(2,128)} %param.15) | copy-start | bytes 196
  3.8 50.4 %all-to-all-start = ((bf16[32,1,8,1024]{3,2,1,0:T(8,128)(2,1)}), bf16[32,1,8,1024]{3,2,1,0:T(8,128)(2,1)S(1)}, u32[]{:S(2)}, u32[]{:S(2)}) async-start(bf16[32,1,8,1024]{3,2,1,0:T(8,128)(2,1)} %copy.84), calls=%async_computation | async-start | bytes 1048576 | tf_op jit(solution)/shard_map/all_to_all | solution.py:89
  56.5 35.9 %all-to-all-start.1 = ((bf16[16,8,8,1024]{3,2,1,0:T(8,128)(2,1)}), bf16[16,8,8,1024]{3,2,1,0:T(8,128)(2,1)}, u32[]{:S(2)}, u32[]{:S(2)}) async-start(bf16[16,8,8,1024]{3,2,1,0:T(8,128)(2,1)} %stack.2), calls=%async_computation.1 | async-start | bytes 4194304 | tf_op jit(solution)/shard_map/all_to_all | solution.py:13
  63.5 37.5 %copy-start.2 = (f32[9,32]{1,0:T(8,128)S(1)}, f32[9,32]{1,0:T(8,128)}, u32[]{:S(2)}) copy-start(f32[9,32]{1,0:T(8,128)} %param.17) | copy-start | bytes 3460
  95.2 5.8 %collective-permute-start = (bf16[1,256,1]{2,1,0:T(8,128)(2,1)S(1)}, bf16[1,256,1]{2,1,0:T(8,128)(2,1)S(1)}, u32[]{:S(2)}, u32[]{:S(2)}) collective-permute-start(bf16[1,256,1]{2,1,0:T(8,128)(2,1)S(1)} %get-tuple-element.254), channel_id=1, source_target_pairs={{0,16},{16,32},{32,48},{48,64},{64,80},{80,96},{96,112},{112,128},... | collective-permute-start | bytes 1544 | tf_op jit(solution)/shard_map/ppermute | solution.py:25
  97.7 5.6 %collective-permute-start.1 = (bf16[1,256,1]{2,1,0:T(8,128)(2,1)S(1)}, bf16[1,256,1]{2,1,0:T(8,128)(2,1)S(1)}, u32[]{:S(2)}, u32[]{:S(2)}) collective-permute-start(bf16[1,256,1]{2,1,0:T(8,128)(2,1)S(1)} %get-tuple-element.253), channel_id=1, source_target_pairs={{16,0},{32,16},{48,32},{64,48},{80,64},{96,80},{112,96},{128,112},... | collective-permute-start | bytes 1544 | tf_op jit(solution)/shard_map/ppermute | solution.py:27
  105.4 8.1 %collective-permute-start.3 = (bf16[1,1,32,256]{3,2,1,0:T(8,128)(2,1)S(1)}, bf16[1,1,32,256]{3,2,1,0:T(8,128)(2,1)}, u32[]{:S(2)}, u32[]{:S(2)}) collective-permute-start(bf16[1,1,32,256]{3,2,1,0:T(8,128)(2,1)S(1)} %maximum_convert_fusion.1), channel_id=1, source_target_pairs={{16,0},{32,16},{48,32},{64,48},{80,64},{96,80},{112,96},{128,112},... | collective-permute-start | bytes 49160 | tf_op jit(solution)/shard_map/ppermute | solution.py:27
  108.1 5.4 %collective-permute-start.2 = (bf16[1,1,32,256]{3,2,1,0:T(8,128)(2,1)S(1)}, bf16[1,1,32,256]{3,2,1,0:T(8,128)(2,1)}, u32[]{:S(2)}, u32[]{:S(2)}) collective-permute-start(bf16[1,1,32,256]{3,2,1,0:T(8,128)(2,1)S(1)} %maximum_convert_fusion.2), channel_id=1, source_target_pairs={{0,16},{16,32},{32,48},{48,64},{64,80},{80,96},{96,112},{112,128},... | collective-permute-start | bytes 49160 | tf_op jit(solution)/shard_map/ppermute | solution.py:25
  137.6 3.2 copy-start.1
  137.6 7.3 %copy-start.3 = (bf16[9,32]{1,0:T(8,128)(2,1)S(1)}, bf16[9,32]{1,0:T(8,128)(2,1)}, u32[]{:S(2)}) copy-start(bf16[9,32]{1,0:T(8,128)(2,1)} %get-tuple-element.413) | copy-start | bytes 1732 | tf_op jit(solution)/shard_map/while
  200.6 3.2 copy-start.1
  200.6 7.3 %copy-start.3 = (bf16[9,32]{1,0:T(8,128)(2,1)S(1)}, bf16[9,32]{1,0:T(8,128)(2,1)}, u32[]{:S(2)}) copy-start(bf16[9,32]{1,0:T(8,128)(2,1)} %get-tuple-element.413) | copy-start | bytes 1732 | tf_op jit(solution)/shard_map/while
  263.6 3.2 copy-start.1
  263.6 7.3 %copy-start.3 = (bf16[9,32]{1,0:T(8,128)(2,1)S(1)}, bf16[9,32]{1,0:T(8,128)(2,1)}, u32[]{:S(2)}) copy-start(bf16[9,32]{1,0:T(8,128)(2,1)} %get-tuple-element.413) | copy-start | bytes 1732 | tf_op jit(solution)/shard_map/while
  326.5 3.2 copy-start.1
  326.5 7.3 %copy-start.3 = (bf16[9,32]{1,0:T(8,128)(2,1)S(1)}, bf16[9,32]{1,0:T(8,128)(2,1)}, u32[]{:S(2)}) copy-start(bf16[9,32]{1,0:T(8,128)(2,1)} %get-tuple-element.413) | copy-start | bytes 1732 | tf_op jit(solution)/shard_map/while
